TPU v7x, 512 devices: a whole 4x8x8 slice. The times are simulated.
512 devices in a mesh: prow: 16 (over z, core), pcol: 32 (over y, x).
Axes of the slice: x: 4, y: 8, z: 8, core: 2. Of those that a mesh axis runs over, the one named last changes fastest.
Arguments:
- hamiltonian: float32 [16384, 16384], P('prow', 'pcol'), may hold values from -60 to 60, as said below
Outputs:
- reduced: float32 [16384, 16384], P('prow', 'pcol')
Inputs may be any that keep to these rules, and one draw needn't show every extreme that they name: hamiltonian holds a symmetric matrix in the stated storage: H[a, b] = H[b, a] exactly.
All inputs are finite; a program needn't handle non-finite values.
Results may differ from a plain program's by a relative error of at most 0.0003.
Values sent between devices are 32-bit elements; how exact they have to be, the bound alone decides.
A program may use at most 64 MiB of HBM per device.

v0:
```python
import jax
import jax.numpy as jnp
from jax import lax
from jax.sharding import PartitionSpec as P

NB = 128


exact_mode = lax.Precision.HIGHEST


def broadcast(block, axis, holder):
    block = jnp.where(lax.axis_index(axis) == holder, block, jnp.zeros_like(block))
    return lax.psum(block, axis)


def product_of(left, right):
    return jnp.dot(left, right, precision=exact_mode, preferred_element_type=jnp.float32)


def inner_product(left, right):
    return lax.dot_general(
        left,
        right,
        (((0,), (0,)), ((), ())),
        precision=exact_mode,
        preferred_element_type=jnp.float32,
    )


def outer_product(left, right):
    return lax.dot_general(
        left,
        right,
        (((1,), (1,)), ((), ())),
        precision=exact_mode,
        preferred_element_type=jnp.float32,
    )


def lower_inverse(gram):
    lower = jnp.linalg.cholesky(gram)
    return jax.scipy.linalg.solve_triangular(
        lower, jnp.eye(gram.shape[0], dtype=jnp.float32), lower=True
    )


def column_copy(rows_array, col_ratio, pick_index):
    width = rows_array.shape[1]
    blocks = rows_array.reshape(rows_array.shape[0] // (col_ratio * NB), col_ratio, NB, width)
    chosen = lax.dynamic_index_in_dim(blocks, pick_index, axis=1, keepdims=False)
    return chosen.reshape(-1, width)


def on_device(hamiltonian):
    rows_dev, cols_dev = hamiltonian.shape
    prow_count = lax.axis_size("prow")
    pcol_count = lax.axis_size("pcol")
    col_ratio = pcol_count // prow_count
    prow_index = lax.axis_index("prow")
    pcol_index = lax.axis_index("pcol")
    pick_index = pcol_index // prow_count
    diagonal_root = pcol_index % prow_count
    local_rows = jnp.arange(rows_dev, dtype=jnp.int32)
    global_rows = (local_rows // NB * prow_count + prow_index) * NB + local_rows % NB
    offsets = jnp.arange(NB, dtype=jnp.int32)
    eye_block = jnp.eye(NB, dtype=jnp.float32)
    matrix = hamiltonian
    for panel_index in range(2):
        col_offset = panel_index // pcol_count * NB
        row_start = (panel_index + 1) * NB
        panel_rows = broadcast(
            matrix[:, col_offset : col_offset + NB], "pcol", panel_index % pcol_count
        )
        panel_rows = jnp.where((global_rows >= row_start)[:, None], panel_rows, jnp.float32(0.0))
        top_offset = (panel_index + 1) // prow_count * NB
        top_term = jnp.where(
            prow_index == (panel_index + 1) % prow_count,
            panel_rows[top_offset : top_offset + NB],
            jnp.float32(0.0),
        )
        gram_panel, top_panel = lax.psum((inner_product(panel_rows, panel_rows), top_term), "prow")
        inverse_second = lower_inverse(gram_panel)
        unit_rows = (global_rows[:, None] == row_start + offsets[None, :]).astype(jnp.float32)
        reflector_vector_rows = outer_product(panel_rows, inverse_second) + unit_rows
        shifted = eye_block + outer_product(top_panel, inverse_second)
        factor = jnp.linalg.cholesky(inner_product(shifted, shifted))
        reflector_coupling = jax.scipy.linalg.cho_solve((factor, True), shifted.T).T
        reflector_vector_cols = broadcast(
            column_copy(reflector_vector_rows, col_ratio, pick_index), "prow", diagonal_root
        )
        image_rows = lax.psum(product_of(matrix, reflector_vector_cols), "pcol")
        mixed_rows = product_of(image_rows, reflector_coupling)
        folded = lax.psum(inner_product(reflector_vector_rows, mixed_rows), "prow")
        correction = inner_product(reflector_coupling, folded)
        weight_rows = mixed_rows - 0.5 * product_of(reflector_vector_rows, correction)
        weight_cols = broadcast(
            column_copy(weight_rows, col_ratio, pick_index), "prow", diagonal_root
        )
        weight_rows, weight_cols = (weight_rows, weight_cols)
        left_side = jnp.concatenate([reflector_vector_rows, weight_rows], axis=1)
        right_side = jnp.concatenate([weight_cols, reflector_vector_cols], axis=1)
        matrix = matrix - outer_product(left_side, right_side)
    return matrix


def solution(mesh):
    return jax.shard_map(
        on_device,
        mesh=mesh,
        in_specs=(P("prow", "pcol"),),
        out_specs=P("prow", "pcol"),
        check_vma=False,
    )
```

profile of v0, /device:TPU:1, one launch (start us, length us, event | category | flops | bytes accessed | tf_op | source)
XLA Modules:
  0.0 1629.6 jit_solution(1243105373318885212)
XLA Ops:
  6.5 1.9 slice_select_fusion.1
  8.6 161.5 %all-reduce.15.cloned.1.call-done = f32[1024,128]{1,0:T(8,128)} async-done(((f32[1024,128]{1,0:T(8,128)}), f32[1024,128]{1,0:T(8,128)}) %all-reduce.15.cloned.1.call-update) | async-done | bytes 524304 | tf_op jit(solution)/shard_map/psum | solution.py:14
  170.1 1.2 broadcast_select_fusion.1
  171.3 1.6 fusion.53
  173.0 0.6 slice_select_fusion.3
  173.6 106.5 %all-reduce.17.cloned.1.call-done = f32[128,128]{0,1:T(8,128)} async-done(((f32[128,128]{0,1:T(8,128)}), f32[128,128]{0,1:T(8,128)}) %all-reduce.17.cloned.1.call-update) | async-done | bytes 65552 | tf_op jit(solution)/shard_map/psum | solution.py:82
  280.1 0.9 copy.3
  281.1 0.9 fusion.39
  281.9 11.7 cholesky.74
  293.7 0.6 compare_reduce_fusion.3
  294.3 0.7 fusion.18
  295.0 9.8 custom-call.14
  305.1 0.6 convolution_add_fusion.1
  305.7 0.7 dynamic-slice_select_fusion.3
  306.6 111.5 %all-reduce.37.cloned.1.call-done = (f32[512,128]{1,0:T(8,128)}, f32[128,128]{1,0:T(8,128)}) async-done(((f32[512,128]{1,0:T(8,128)}, f32[128,128]{1,0:T(8,128)}), (f32[512,128]{1,0:T(8,128)}, f32[128,128]{1,0:T(8,128)})) %all-reduce.37.cloned.1.call-update) | async-done | bytes 327696 | tf_op jit(solution)/shard_map/psum | solution.py:14
  418.1 1.1 fusion.54
  419.2 0.3 fusion.24
  419.6 11.7 cholesky.85
  431.4 0.7 compare_reduce_fusion.2
  432.1 4.1 convolution_bitcast_fusion
  436.2 0.6 fusion.19
  436.9 9.8 custom-call.15
  447.2 142.0 %all-reduce.19.cloned.1.call-done = f32[1024,128]{0,1:T(8,128)} async-done(((f32[1024,128]{0,1:T(8,128)}), f32[1024,128]{0,1:T(8,128)}) %all-reduce.19.cloned.1.call-update) | async-done | bytes 524304 | tf_op jit(solution)/shard_map/psum | solution.py:92
  589.2 2.0 fusion.55
  591.3 1.6 fusion.56
  593.0 106.9 %all-reduce.21.cloned.1.call-done = f32[128,128]{1,0:T(8,128)} async-done(((f32[128,128]{1,0:T(8,128)}), f32[128,128]{1,0:T(8,128)}) %all-reduce.21.cloned.1.call-update) | async-done | bytes 65552 | tf_op jit(solution)/shard_map/psum | solution.py:94
  699.9 1.0 fusion.57
  701.0 0.6 fusion.1
  701.5 0.7 dynamic-slice_select_fusion.2
  702.6 112.6 %all-reduce.23.cloned.1.call-done = f32[512,128]{1,0:T(8,128)} async-done(((f32[512,128]{1,0:T(8,128)}), f32[512,128]{1,0:T(8,128)}) %all-reduce.23.cloned.1.call-update) | async-done | bytes 262160 | tf_op jit(solution)/shard_map/psum | solution.py:14
  815.2 3.5 convolution_subtract_fusion.1
  818.7 0.9 slice_select_fusion
  819.7 153.6 %all-reduce.25.cloned.1.call-done = f32[1024,128]{1,0:T(8,128)} async-done(((f32[1024,128]{1,0:T(8,128)}), f32[1024,128]{1,0:T(8,128)}) %all-reduce.25.cloned.1.call-update) | async-done | bytes 524304 | tf_op jit(solution)/shard_map/psum | solution.py:14
  973.3 1.2 broadcast_select_fusion
  974.5 1.6 fusion.58
  976.2 0.6 slice_select_fusion.2
  976.8 106.3 %all-reduce.27.cloned.1.call-done = f32[128,128]{0,1:T(8,128)} async-done(((f32[128,128]{0,1:T(8,128)}), f32[128,128]{0,1:T(8,128)}) %all-reduce.27.cloned.1.call-update) | async-done | bytes 65552 | tf_op jit(solution)/shard_map/psum | solution.py:82
  1083.2 0.9 copy.6
  1084.1 0.9 fusion.32
  1084.9 11.7 cholesky.96
  1096.7 0.6 compare_reduce_fusion.1
  1097.3 0.7 fusion.20
  1098.0 9.8 custom-call.17
  1108.1 0.6 convolution_add_fusion
  1108.7 0.7 dynamic-slice_select_fusion.1
  1109.4 0.3 all-reduce.29.cloned.1.call-start
  1109.7 111.4 %all-reduce.35.cloned.1.call-done = (f32[512,128]{1,0:T(8,128)}, f32[128,128]{1,0:T(8,128)}) async-done(((f32[512,128]{1,0:T(8,128)}, f32[128,128]{1,0:T(8,128)}), (f32[512,128]{1,0:T(8,128)}, f32[128,128]{1,0:T(8,128)})) %all-reduce.35.cloned.1.call-update) | async-done | bytes 327696 | tf_op jit(solution)/shard_map/psum | solution.py:14
  1221.1 1.1 fusion.60
  1222.7 11.7 cholesky.107
  1234.4 0.7 compare_reduce_fusion
  1235.1 3.5 fusion.59
  1238.7 0.6 fusion.21
  1239.4 9.8 custom-call.18
  1249.7 142.0 %all-reduce.29.cloned.1.call-done = f32[1024,128]{1,0:T(8,128)} async-done(((f32[1024,128]{1,0:T(8,128)}), f32[1024,128]{1,0:T(8,128)}) %all-reduce.29.cloned.1.call-update) | async-done | bytes 524304 | tf_op jit(solution)/shard_map/psum | solution.py:92
  1391.7 1.6 fusion.61
  1393.3 1.6 fusion.62
  1395.0 0.3 all-reduce.33.cloned.1.call-start
  1395.3 106.6 %all-reduce.31.cloned.1.call-done = f32[128,128]{1,0:T(8,128)} async-done(((f32[128,128]{1,0:T(8,128)}), f32[128,128]{1,0:T(8,128)}) %all-reduce.31.cloned.1.call-update) | async-done | bytes 65552 | tf_op jit(solution)/shard_map/psum | solution.py:94
  1502.0 1.0 fusion.63
  1503.0 0.6 fusion
  1503.6 0.8 copy-done.1
  1504.4 0.7 dynamic-slice_select_fusion
  1505.1 112.9 %all-reduce.33.cloned.1.call-done = f32[512,128]{1,0:T(8,128)} async-done(((f32[512,128]{1,0:T(8,128)}), f32[512,128]{1,0:T(8,128)}) %all-reduce.33.cloned.1.call-update) | async-done | bytes 262160 | tf_op jit(solution)/shard_map/psum | solution.py:14
  1618.0 4.3 convolution_subtract_fusion
  (49 shorter events, 3.2 us)
Async XLA Ops:
  6.5 163.5 %all-reduce.15.cloned.1.call-start = ((), (), s32[]{:S(2)}) async-start(), calls=%async_computation | async-start | bytes 1048576 | tf_op jit(solution)/shard_map/psum | solution.py:14
  8.4 271.7 %all-reduce.17.cloned.1.call-start = ((), (), s32[]{:S(2)}) async-start(), calls=%async_computation.1 | async-start | bytes 131072 | tf_op jit(solution)/shard_map/psum | solution.py:82
  171.3 260.8 %copy-start = (f32[1024,512]{1,0:T(8,128)S(1)}, f32[1024,512]{1,0:T(8,128)}, u32[]{:S(2)}) copy-start(f32[1024,512]{1,0:T(8,128)} %param.6) | copy-start | bytes 6291460
  173.0 245.2 %all-reduce.37.cloned.1.call-start = ((), (), s32[]{:S(2)}) async-start(), calls=%async_computation.11 | async-start | bytes 655360 | tf_op jit(solution)/shard_map/psum | solution.py:14
  306.4 282.8 %all-reduce.19.cloned.1.call-start = ((), (), s32[]{:S(2)}) async-start(), calls=%async_computation.2 | async-start | bytes 1048576 | tf_op jit(solution)/shard_map/psum | solution.py:92
  436.2 263.7 %all-reduce.21.cloned.1.call-start = ((), (), s32[]{:S(2)}) async-start(), calls=%async_computation.3 | async-start | bytes 131072 | tf_op jit(solution)/shard_map/psum | solution.py:94
  591.3 223.9 %copy-start.2 = (f32[512,128]{1,0:T(8,128)S(1)}, f32[512,128]{1,0:T(8,128)}, u32[]{:S(2)}) copy-start(f32[512,128]{1,0:T(8,128)} %get-tuple-element.10) | copy-start | bytes 786436
  592.9 222.2 %all-reduce.23.cloned.1.call-start = ((), (), s32[]{:S(2)}) async-start(), calls=%async_computation.4 | async-start | bytes 524288 | tf_op jit(solution)/shard_map/psum | solution.py:14
  702.3 271.0 %all-reduce.25.cloned.1.call-start = ((), (), s32[]{:S(2)}) async-start(), calls=%async_computation.5 | async-start | bytes 1048576 | tf_op jit(solution)/shard_map/psum | solution.py:14
  819.6 263.6 %all-reduce.27.cloned.1.call-start = ((), (), s32[]{:S(2)}) async-start(), calls=%async_computation.6 | async-start | bytes 131072 | tf_op jit(solution)/shard_map/psum | solution.py:82
  976.2 245.0 %all-reduce.35.cloned.1.call-start = ((), (), s32[]{:S(2)}) async-start(), calls=%async_computation.10 | async-start | bytes 655360 | tf_op jit(solution)/shard_map/psum | solution.py:14
  1109.4 282.3 %all-reduce.29.cloned.1.call-start = ((), (), s32[]{:S(2)}) async-start(), calls=%async_computation.7 | async-start | bytes 1048576 | tf_op jit(solution)/shard_map/psum | solution.py:92
  1238.7 263.3 %all-reduce.31.cloned.1.call-start = ((), (), s32[]{:S(2)}) async-start(), calls=%async_computation.8 | async-start | bytes 131072 | tf_op jit(solution)/shard_map/psum | solution.py:94
  1393.3 224.7 %copy-start.3 = (f32[512,128]{1,0:T(8,128)S(1)}, f32[512,128]{1,0:T(8,128)}, u32[]{:S(2)}) copy-start(f32[512,128]{1,0:T(8,128)} %get-tuple-element.6) | copy-start | bytes 786436
  1395.0 223.0 %all-reduce.33.cloned.1.call-start = ((), (), s32[]{:S(2)}) async-start(), calls=%async_computation.9 | async-start | bytes 524288 | tf_op jit(solution)/shard_map/psum | solution.py:14
  1503.6 0.8 copy-start.1
Sparse Core Ops, SparseCore 0:
  10.7 159.2 all-reduce.14
  173.1 106.9 all-reduce.16
  306.5 111.5 all-reduce.36
  436.3 152.8 all-reduce.18
  593.1 106.8 all-reduce.20
  702.4 112.6 all-reduce.22
  819.7 153.5 all-reduce.24
  976.3 106.8 all-reduce.26
  1109.6 111.5 all-reduce.34
  1238.8 152.8 all-reduce.28
  1395.1 106.8 all-reduce.30
  1505.3 112.6 all-reduce.32
where the time goes:
time: 1640 us; the launch traced here: 1630 us
  waiting for transfers between devices  1470 us (90%)
  other arithmetic  103 us (6%)
  matrix products  34.3 us (2%)
    psum x6, waiting for transfers between devices, broadcast(): return lax.psum(block, axis)  763 us
    psum x2, waiting for transfers between devices, on_device(): image_rows = lax.psum(product_of(matrix, reflector_vector_cols), 'pcol')  284 us
    psum x2, waiting for transfers between devices, on_device(): folded = lax.psum(inner_product(reflector_vector_rows, mixed_rows), 'prow')  214 us
    psum x2, waiting for transfers between devices, on_device(): lax.psum((inner_product(panel_rows, panel_rows), top_term), 'prow')  213 us
  transfers between devices with their start and end apart: 12, of which 12 were waited for; matrix products, arithmetic and copies ran while one was open for 1% of the time, Pallas kernels for 0%

commit v1 on v0

v1 whole, which is shorter than its diff:
```python
import functools

import jax
import jax.numpy as jnp
from jax import lax
from jax.experimental import pallas as pl
from jax.experimental.pallas import tpu as pltpu
from jax.sharding import PartitionSpec as P

NB = 128
PR = 16
PC = 32
NY = 8
NX = 4
CD = 512
SL = NB // PR

MESH = pl.DeviceIdType.MESH
exact_mode = lax.Precision.HIGHEST

SC_P, SC_E, B_P, B_E, G_P, G_E, RS, B_Y, G_Y, C_P, C_E, C_Y, A_RS, A_AG, Q_RS, Q_AG = range(16)


def dot_nn(a, b):
    return lax.dot_general(
        a, b, (((1,), (0,)), ((), ())), precision=exact_mode, preferred_element_type=jnp.float32
    )


def dot_nt(a, b):
    return lax.dot_general(
        a, b, (((1,), (1,)), ((), ())), precision=exact_mode, preferred_element_type=jnp.float32
    )


def dot_tn(a, b):
    return lax.dot_general(
        a, b, (((0,), (0,)), ((), ())), precision=exact_mode, preferred_element_type=jnp.float32
    )


def exchange_kernel(
    j,
    h_ref,
    pr,
    er,
    yr,
    pc,
    ec,
    yc,
    small,
    quad,
    part,
    rs_buf,
    ar_src,
    ar_buf,
    q_src,
    q_buf,
    send_sem,
    recv_sem,
):
    i = lax.axis_index("prow")
    k = lax.axis_index("pcol")
    y = k // NX
    x = k % NX
    half = x // 2
    f_mine = (x % 2) * NY + y
    k_mine = i + PR * half
    home = k_mine == k
    mine = pl.ds(pl.multiple_of(f_mine * SL, SL), SL)

    def holder(f):
        return (k % PR, NX * (f % NY) + 2 * (k // PR) + f // NY)

    def send(src, dst, which, target):
        pltpu.make_async_remote_copy(
            src_ref=src,
            dst_ref=dst,
            send_sem=send_sem.at[which],
            recv_sem=recv_sem.at[which],
            device_id=target,
            device_id_type=MESH,
        ).start()

    def send_or_copy(src, dst, which, target):
        same = jnp.logical_and(target[0] == i, target[1] == k)

        @pl.when(same)
        def _():
            pltpu.make_async_copy(src, dst, recv_sem.at[which]).start()

        @pl.when(jnp.logical_not(same))
        def _():
            send(src, dst, which, target)

    def loop(n, body):
        lax.fori_loop(0, n, lambda t, c: (body(t), c)[1], 0)

    def wait_recv(which, ref):
        pltpu.make_async_copy(ref, ref, recv_sem.at[which]).wait()

    def wait_send(which, ref):
        pltpu.make_async_copy(ref, ref, send_sem.at[which]).wait()

    barrier = pltpu.get_barrier_semaphore()

    def greet(target):
        same = jnp.logical_and(target[0] == i, target[1] == k)

        @pl.when(jnp.logical_not(same))
        def _():
            pl.semaphore_signal(barrier, inc=1, device_id=target, device_id_type=MESH)

    loop(PR, lambda t: greet(holder(t)))
    loop(PR, lambda t: greet((t, k_mine)))
    loop(NY - 1, lambda t: greet((i, NX * lax.rem(y + 1 + t, NY) + x)))
    loop(NX - 1, lambda t: greet((i, NX * y + lax.rem(x + 1 + t, NX))))
    loop(PR - 1, lambda t: greet((lax.rem(i + 1 + t, PR), k)))
    others = (NY - 1) + (NX - 1) + (PR - 1)

    @pl.when(home)
    def _():
        pl.semaphore_wait(barrier, others + 2 * (PR - 1))

    @pl.when(jnp.logical_not(home))
    def _():
        pl.semaphore_wait(barrier, others + 2 * PR)

    def scatter(dst, which):
        def body(t):
            rows = pl.ds(pl.multiple_of(t * SL, SL), SL)
            send_or_copy(h_ref.at[rows, :], dst.at[k // PR, rows, :], which, holder(t))

        loop(PR, body)

    def along_y(ref, which):
        def body(t):
            piece = ref.at[half, mine, :]
            send(piece, piece, which, (i, NX * lax.rem(y + 1 + t, NY) + x))

        loop(NY - 1, body)

    def along_x(ref, which):
        def body(t):
            run = ref.at[half, pl.ds(pl.multiple_of((x % 2) * (NB // 2), NB // 2), NB // 2), :]
            send(run, run, which, (i, NX * y + lax.rem(x + 1 + t, NX)))

        loop(NX - 1, body)

    def to_column(ref, dst, which):
        def body(t):
            send_or_copy(ref.at[half, mine, :], dst.at[mine, :], which, (t, k_mine))

        loop(PR, body)

    def got_y(ref, which):
        wait_recv(which, ref.at[0, pl.ds(0, (NY - 1) * SL), :])

    def got_x(ref, which):
        wait_recv(which, ref.at[:, pl.ds(0, 3 * NB // 4), :])

    @pl.when(i == j)
    def _():
        scatter(pr, SC_P)

    @pl.when(i == j + 1)
    def _():
        scatter(er, SC_E)

    wait_recv(SC_P, pr.at[half, mine, :])
    along_y(pr, B_P)
    wait_recv(SC_E, er.at[half, mine, :])
    along_y(er, B_E)
    got_y(pr, B_P)
    along_x(pr, G_P)
    to_column(pr, pc, C_P)
    got_x(pr, G_P)

    def panel_block(m):
        block = pr[m % 2, :, NB * (m // 2) : NB * (m // 2) + NB]
        if m == 0:
            block = jnp.where(i <= j, jnp.float32(0.0), block)
        return block

    product = dot_nn(panel_block(0), h_ref[0:NB, :])
    for m in range(1, 8):
        product += dot_nn(panel_block(m), h_ref[NB * m : NB * m + NB, :])
    part[...] = product

    def rs_body(t):
        rows = pl.ds(pl.multiple_of(t * SL, SL), SL)
        send_or_copy(part.at[rows, :], rs_buf.at[i], RS, holder(t))

    loop(PR, rs_body)

    gram = jnp.zeros((NB, NB), jnp.float32)
    for m in range(8):
        gram += dot_nt(panel_block(m), panel_block(m))
    ar_src[0] = gram

    got_y(er, B_E)
    along_x(er, G_E)
    to_column(er, ec, C_E)

    wait_recv(RS, rs_buf)
    total = rs_buf[0]
    for t in range(1, PR):
        total += rs_buf[t]
    yr[half, mine, :] = total
    along_y(yr, B_Y)
    to_column(yr, yc, C_Y)

    got_x(er, G_E)

    def cross(ref):
        total = jnp.zeros((NB, NB), jnp.float32)
        for m in range(8):
            total += dot_nt(
                panel_block(m), ref[m % 2, :, NB * (m // 2) : NB * (m // 2) + NB]
            )
        return total

    ar_src[1] = cross(er)
    ar_src[2] = jnp.where(i == j + 1, pr[0, :, 0:NB], jnp.float32(0.0))
    ar_src[3] = jnp.where(i == j + 1, er[0, :, 0:NB], jnp.float32(0.0))

    def ar_body(t):
        rows = pl.ds(pl.multiple_of(t * SL, SL), SL)
        send_or_copy(ar_src.at[:, rows, :], ar_buf.at[i], A_RS, (t, k))

    loop(PR, ar_body)

    got_y(yr, B_Y)
    along_x(yr, G_Y)

    own = pl.ds(pl.multiple_of(i * SL, SL), SL)
    wait_recv(A_RS, ar_buf)
    total = ar_buf[0]
    for t in range(1, PR):
        total += ar_buf[t]
    small[:, own, :] = total

    def ag_body(t):
        send(small.at[:, own, :], small.at[:, own, :], A_AG, (lax.rem(i + 1 + t, PR), k))

    loop(PR - 1, ag_body)

    got_x(yr, G_Y)
    q_src[...] = cross(yr)

    def q_body(t):
        rows = pl.ds(pl.multiple_of(t * SL, SL), SL)
        send_or_copy(q_src.at[rows, :], q_buf.at[i], Q_RS, (t, k))

    loop(PR, q_body)
    wait_recv(Q_RS, q_buf)
    total = q_buf[0]
    for t in range(1, PR):
        total += q_buf[t]
    quad[own, :] = total

    def qg_body(t):
        send(quad.at[own, :], quad.at[own, :], Q_AG, (lax.rem(i + 1 + t, PR), k))

    loop(PR - 1, qg_body)

    wait_recv(C_P, pc)
    wait_recv(C_E, ec)
    wait_recv(C_Y, yc)
    wait_recv(A_AG, small.at[:, pl.ds(0, NB - SL), :])
    wait_recv(Q_AG, quad.at[pl.ds(0, NB - SL), :])

    def sent_pieces(which):
        @pl.when(home)
        def _():
            wait_send(which, pr.at[0, pl.ds(0, NB - SL), :])

        @pl.when(jnp.logical_not(home))
        def _():
            wait_send(which, pr.at[0])

    @pl.when(i == j)
    def _():
        sent_pieces(SC_P)

    @pl.when(i == j + 1)
    def _():
        sent_pieces(SC_E)

    for which in (RS, C_P, C_E, C_Y):
        sent_pieces(which)
    for which in (B_P, B_E, B_Y):
        wait_send(which, pr.at[0, pl.ds(0, (NY - 1) * SL), :])
    for which in (G_P, G_E, G_Y):
        wait_send(which, pr.at[:, pl.ds(0, 3 * NB // 4), :])
    for which in (A_RS, A_AG):
        wait_send(which, small.at[:, pl.ds(0, NB - SL), :])
    for which in (Q_RS, Q_AG):
        wait_send(which, quad.at[pl.ds(0, NB - SL), :])


def exchange(j, matrix):
    f32 = jnp.float32
    vmem = pl.BlockSpec(memory_space=pltpu.VMEM)
    rows = jax.ShapeDtypeStruct((2, NB, CD), f32)
    cols = jax.ShapeDtypeStruct((NB, CD), f32)
    return pl.pallas_call(
        functools.partial(exchange_kernel, j),
        out_shape=(
            rows,
            rows,
            rows,
            cols,
            cols,
            cols,
            jax.ShapeDtypeStruct((4, NB, NB), f32),
            jax.ShapeDtypeStruct((NB, NB), f32),
        ),
        in_specs=[vmem],
        out_specs=(vmem,) * 8,
        scratch_shapes=[
            pltpu.VMEM((NB, CD), f32),
            pltpu.VMEM((PR, SL, CD), f32),
            pltpu.VMEM((4, NB, NB), f32),
            pltpu.VMEM((PR, 4, SL, NB), f32),
            pltpu.VMEM((NB, NB), f32),
            pltpu.VMEM((PR, SL, NB), f32),
            pltpu.SemaphoreType.DMA((16,)),
            pltpu.SemaphoreType.DMA((16,)),
        ],
        compiler_params=pltpu.CompilerParams(
            collective_id=j, has_side_effects=True, vmem_limit_bytes=32 * 1024 * 1024
        ),
        name=f"exchange_{j}",
    )(matrix)


def lower_inverse(gram):
    lower = jnp.linalg.cholesky(gram)
    return jax.scipy.linalg.solve_triangular(
        lower, jnp.eye(gram.shape[0], dtype=jnp.float32), lower=True
    )


def on_device(matrix):
    i = lax.axis_index("prow")
    k = lax.axis_index("pcol")
    eye = jnp.eye(NB, dtype=jnp.float32)
    first = (jnp.arange(CD) < NB)[None, :]
    unit = jnp.concatenate([eye, jnp.zeros((NB, CD - NB), jnp.float32)], axis=1)
    for j in range(2):
        pr, er, yr, pc, ec, yc, small, quad = exchange(j, matrix)
        gram, cross, top_t, corner = small[0], small[1], small[2], small[3]
        inverse_second = lower_inverse(gram)
        shifted = eye + dot_tn(top_t, inverse_second.T)
        factor = jnp.linalg.cholesky(dot_tn(shifted, shifted))
        coupling = jax.scipy.linalg.cho_solve((factor, True), shifted.T).T
        mixed = dot_nn(inverse_second, cross)
        inner = dot_nt(dot_nn(inverse_second, quad), inverse_second) + mixed + mixed.T + corner
        middle = dot_tn(coupling, dot_nn(inner, coupling))

        def factors(p, e, yv, index):
            p = jnp.where(jnp.logical_and(first, index <= j), jnp.float32(0.0), p)
            vectors = dot_nn(inverse_second, p)
            vectors += jnp.where(index == j + 1, unit, jnp.float32(0.0))
            image = dot_nn(inverse_second, yv) + e
            weights = dot_tn(coupling, image) - 0.5 * dot_tn(middle, vectors)
            return vectors, weights

        v0, w0 = factors(pr[0], er[0], yr[0], i)
        v1, w1 = factors(pr[1], er[1], yr[1], PR + k * 0)
        vc, wc = factors(pc, ec, yc, k)
        left = jnp.stack([jnp.concatenate([v0, w0]), jnp.concatenate([v1, w1])])
        left = left.reshape(2, 2 * NB, 4, NB).transpose(1, 2, 0, 3).reshape(2 * NB, 8 * NB)
        right = jnp.concatenate([wc, vc])
        matrix = matrix - dot_tn(left, right)
    return matrix


def solution(mesh):
    return jax.shard_map(
        on_device,
        mesh=mesh,
        in_specs=(P("prow", "pcol"),),
        out_specs=P("prow", "pcol"),
        check_vma=False,
    )
```

time: 1640 us -> 484 us (0.30)
  waiting for transfers between devices: 1470 us -> 0 us
  Pallas kernels: 0 us -> 325 us
    psum x12 -> x0, waiting for transfers between devices: 1470 us -> none  [the longest x6 763 us: broadcast(): return lax.psum(block, axis)]
    pallas_call x0 -> x2, Pallas kernels: none -> 325 us  [exchange(): pl.pallas_call(functools.partial(exchange_kernel, j), out_shape=(rows, ro...]
    another operation x10 -> x12, other arithmetic: 45.8 us -> 49.9 us  [the longest x6 25.7 us: on_device(): factor = jnp.linalg.cholesky(dot_tn(shifted, shifted))]
  transfers between devices with their start and end apart: 12 -> 0, of which waited for: 12 -> 0; matrix products, arithmetic and copies ran while one was open for 1% -> 0% of each run, Pallas kernels for 0% -> 0%
where the time goes in v1:
time: 484 us; the launch traced here: 478 us
  Pallas kernels  325 us (67%)
  other arithmetic  103 us (21%)
  matrix products  33.7 us (7%)
  local copies, waits for them, and re-layouts  15.6 us (3%)
    pallas_call x2, Pallas kernels, exchange(): pl.pallas_call(functools.partial(exchange_kernel, j), out_shape=(rows, ro...  325 us
    another operation x6, other arithmetic, on_device(): factor = jnp.linalg.cholesky(dot_tn(shifted, shifted))  25.7 us
    another operation x6, other arithmetic, lower_inverse(): lower = jnp.linalg.cholesky(gram)  25.6 us
    another operation x4, other arithmetic, lower_inverse(): jax.scipy.linalg.solve_triangular(lower, jnp.eye(gram.shape[0], dtype=jnp...  23 us
    another operation x4, other arithmetic, on_device(): coupling = jax.scipy.linalg.cho_solve((factor, True), shifted.T).T  22.9 us
    dot_general x20, matrix products, dot_tn(): lax.dot_general(a, b, (((0,), (0,)), ((), ())), precision=exact_mode, pre...  16.9 us
    dot_general x18, matrix products, dot_nn(): lax.dot_general(a, b, (((1,), (0,)), ((), ())), precision=exact_mode, pre...  11.2 us

profile of v1, /device:TPU:1, one launch (start us, length us, event | category | flops | bytes accessed | tf_op | source)
XLA Modules:
  0.0 477.6 jit_solution(17354872303321965316)
XLA Ops:
  0.1 1.6 copy-done
  1.7 168.8 %exchange_0.1 = (f32[2,128,512]{2,1,0:T(8,128)S(1)}, f32[2,128,512]{2,1,0:T(8,128)S(1)}, f32[2,128,512]{2,1,0:T(8,128)S(1)}, f32[128,512]{1,0:T(8,128)S(1)}, f32...) custom-call(f32[1024,512]{1,0:T(8,128)S(1)} %copy-done), custom_call_target="tpu_custom_call" | custom-call | tf_op jit(solution)/shard_map/exchange_0/pallas_call | solution.py:307
  170.8 11.7 %cholesky.74 = f32[128,128]{1,0:T(8,128)S(1)} custom-call(f32[128,128]{1,0:T(8,128)S(1)} %fusion.55), custom_call_target="Cholesky" | custom-call | tf_op jit(solution)/shard_map/jit(cholesky)/cholesky | solution.py:339
  182.5 0.6 compare_reduce_fusion.3
  183.2 0.7 fusion.46
  183.8 9.8 %custom-call.14 = f32[1,128,128]{1,2,0:T(8,128)S(1)} custom-call(f32[1,128,128]{2,1,0:T(8,128)S(1)} %fusion.46), custom_call_target="InvertDiagBlocksLowerTriangular" | custom-call | tf_op jit(solution)/shard_map/jit(_solve_triangular)/triangular_solve/custom-call.0 | solution.py:340
  193.9 0.4 convolution_add_fusion.6
  194.3 0.4 convolution_add_fusion.5
  195.8 11.7 %cholesky.85 = f32[128,128]{1,0:T(8,128)S(1)} custom-call(f32[128,128]{1,0:T(8,128)S(1)} %fusion.71), custom_call_target="Cholesky" | custom-call | tf_op jit(solution)/shard_map/jit(cholesky)/cholesky | solution.py:356
  207.6 0.6 compare_reduce_fusion.2
  208.2 0.7 fusion.47
  208.9 10.2 %custom-call.15 = f32[1,128,128]{1,2,0:T(8,128)S(1)} custom-call(f32[1,128,128]{2,1,0:T(8,128)S(1)} %fusion.47), custom_call_target="InvertDiagBlocksLowerTriangular" | custom-call | tf_op jit(solution)/shard_map/jit(_cho_solve)/triangular_solve | solution.py:357
  219.6 0.4 fusion.96
  220.8 0.4 fusion.3
  221.2 0.4 convolution_add_fusion.9
  222.0 0.4 convolution_add_fusion.7
  222.4 0.4 convolution_add_fusion.8
  223.5 0.4 fusion.4
  223.9 0.4 fusion.5
  224.9 3.4 convolution_subtract_fusion.1.h_ref
  228.3 155.9 %exchange_1.1 = (f32[2,128,512]{2,1,0:T(8,128)S(1)}, f32[2,128,512]{2,1,0:T(8,128)S(1)}, f32[2,128,512]{2,1,0:T(8,128)S(1)}, f32[128,512]{1,0:T(8,128)S(1)}, f32...) custom-call(f32[1024,512]{1,0:T(8,128)S(1)} %convolution_subtract_fusion.1.h_ref), custom_call_target="tpu_custom_call" | custom-call | tf_op jit(solution)/shard_map/exchange_1/pallas_call | solution.py:307
  384.3 0.8 copy-done.1
  385.1 0.7 copy-done.3
  385.8 0.7 copy-done.4
  386.5 0.7 copy-done.5
  387.2 0.8 copy.19
  388.0 1.5 slice_bitcast_fusion
  389.4 0.9 copy.20
  390.4 1.5 fusion.54
  391.9 12.5 %cholesky.96 = f32[128,128]{1,0:T(8,128)S(1)} custom-call(f32[128,128]{1,0:T(8,128)} %fusion.54), custom_call_target="Cholesky" | custom-call | tf_op jit(solution)/shard_map/jit(cholesky)/cholesky | solution.py:339
  404.4 0.7 compare_reduce_fusion.1
  405.1 1.2 fusion.48
  406.3 11.3 %custom-call.17 = f32[1,128,128]{1,2,0:T(8,128)} custom-call(f32[1,128,128]{2,1,0:T(8,128)} %fusion.48), custom_call_target="InvertDiagBlocksLowerTriangular" | custom-call | tf_op jit(solution)/shard_map/jit(_solve_triangular)/triangular_solve/custom-call.0 | solution.py:340
  417.6 1.1 fusion.42
  418.7 2.1 convolution_add_fusion.1
  420.8 2.0 convolution_add_fusion
  422.9 0.8 fusion.98
  423.7 0.8 fusion.56
  424.8 0.6 copy-done.11
  425.7 1.6 copy.22
  427.3 0.7 copy.21
  428.0 1.5 fusion.62
  429.5 12.5 %cholesky.107 = f32[128,128]{1,0:T(8,128)S(1)} custom-call(f32[128,128]{1,0:T(8,128)} %fusion.62), custom_call_target="Cholesky" | custom-call | tf_op jit(solution)/shard_map/jit(cholesky)/cholesky | solution.py:356
  442.1 0.7 compare_reduce_fusion
  442.8 1.3 fusion.49
  444.0 10.8 %custom-call.18 = f32[1,128,128]{1,2,0:T(8,128)S(1)} custom-call(f32[1,128,128]{2,1,0:T(8,128)} %fusion.49), custom_call_target="InvertDiagBlocksLowerTriangular" | custom-call | tf_op jit(solution)/shard_map/jit(_cho_solve)/triangular_solve | solution.py:357
  454.9 0.6 copy-done.12
  455.5 1.1 fusion.51
  456.6 1.0 fusion.60
  457.6 2.0 fusion.102
  459.7 1.6 copy.23
  461.2 1.2 fusion.7
  462.9 2.2 fusion
  465.1 1.2 convolution_add_fusion.4
  466.7 0.4 convolution_add_fusion.2
  467.1 0.4 convolution_add_fusion.3
  467.9 0.4 fusion.101
  468.2 1.1 fusion.1
  469.4 0.4 fusion.2
  469.9 1.0 copy.28
  470.9 1.0 pad_maximum_fusion.5
  471.9 1.0 copy.29
  472.9 1.3 pad_maximum_fusion.1
  474.2 3.1 convolution_subtract_fusion
  (61 shorter events, 6.6 us)
Async XLA Ops:
  0.1 1.6 copy-start
  1.7 219.6 %copy-start.9 = (f32[128,128]{1,0:T(8,128)}, f32[128,128]{1,0:T(8,128)S(1)}, u32[]{:S(2)}) copy-start(f32[128,128]{1,0:T(8,128)S(1)} %fusion.76) | copy-start | bytes 196612
  384.3 0.8 copy-start.1
  385.1 0.7 copy-start.3
  385.8 0.7 copy-start.4
  386.5 0.7 copy-start.5
  424.8 0.6 copy-start.11
  454.8 0.6 copy-start.12
  461.2 5.5 %copy-start.2 = (f32[2,128,512]{2,1,0:T(8,128)S(1)}, f32[2,128,512]{2,1,0:T(8,128)}, u32[]{:S(2)}) copy-start(f32[2,128,512]{2,1,0:T(8,128)} %copy-done.1) | copy-start | bytes 1572868
  466.7 1.5 copy-start.7
  469.4 1.5 copy-start.8
  470.8 3.3 copy-start.6
  470.9 3.3 copy-start.10

commit v2 on v0

v2 whole, which is shorter than its diff:
```python
import jax
import jax.numpy as jnp
from jax import lax
from jax.experimental import pallas as pl
from jax.experimental.pallas import tpu as pltpu
from jax.sharding import PartitionSpec as P

NB = 128
PR = 16
NZ = 8
NY = 8
NX = 4
CD = 512
SL = NB // PR
HF = NB // 2

MESH = pl.DeviceIdType.MESH
f32 = jnp.float32
exact_mode = lax.Precision.HIGHEST


def dot_nn(a, b):
    return lax.dot_general(
        a, b, (((1,), (0,)), ((), ())), precision=exact_mode, preferred_element_type=f32
    )


def dot_nt(a, b):
    return lax.dot_general(
        a, b, (((1,), (1,)), ((), ())), precision=exact_mode, preferred_element_type=f32
    )


def dot_tn(a, b):
    return lax.dot_general(
        a, b, (((0,), (0,)), ((), ())), precision=exact_mode, preferred_element_type=f32
    )


def eliminate(first, last, w_ref, g_ref, linv_ref, r_ref):
    lane = lax.broadcasted_iota(jnp.int32, (8, NB), 1)
    sub = lax.broadcasted_iota(jnp.int32, (8, NB), 0)
    zero = jnp.zeros((8, NB), f32)

    def body(b, carry):
        w, g = list(carry[:16]), list(carry[16:])
        left = NB - 8 * b
        scale = zero
        for s in range(8):
            here = lane == s
            row = jnp.broadcast_to(w[0][s : s + 1, :], (8, NB))
            d = jnp.broadcast_to(row[:, s : s + 1], (8, NB))
            rs = lax.rsqrt(d)
            scale = jnp.where(sub == s, rs, scale)
            rd = rs * rs
            step = jnp.where(here, rd, row * rd)
            grow = jnp.broadcast_to(g[0][s : s + 1, :], (8, NB))
            grow = grow + jnp.where(jnp.logical_and(lane >= s, lane < left), row * rs, 0.0)
            gd = 1.0 / jnp.broadcast_to(grow[:, s : s + 1], (8, NB))
            gstep = jnp.where(here, gd, grow * gd)
            for v in range(16):
                wc = jnp.broadcast_to(w[v][:, s : s + 1], (8, NB))
                gc = jnp.broadcast_to(g[v][:, s : s + 1], (8, NB))
                if v == 0:
                    w[0] = jnp.where(sub > s, jnp.where(here, 0.0, w[0]) - wc * step, w[0])
                    g[0] = jnp.where(sub == s, gstep, jnp.where(here, 0.0, g[0]) - gc * gstep)
                else:
                    w[v] = jnp.where(here, 0.0, w[v]) - wc * step
                    g[v] = jnp.where(here, 0.0, g[v]) - gc * gstep
        lower = jnp.logical_or(lane >= left, lane < sub)
        linv = scale * jnp.where(lower, w[0], jnp.where(lane == sub, 1.0, 0.0))
        upper = scale * jnp.where(lower, 0.0, w[0])
        rows = pl.ds(pl.multiple_of(8 * b, 8), 8)
        linv_ref[rows, :] = pltpu.roll(linv, 8 * b, 1)
        r_ref[rows, :] = pltpu.roll(upper, 8 * b, 1)
        w = [pltpu.roll(t, NB - 8, 1) for t in w[1:]] + [zero]
        g = [pltpu.roll(t, NB - 8, 1) for t in g[1:] + g[:1]]
        return tuple(w + g)

    init = tuple(w_ref[8 * v : 8 * v + 8, :] for v in range(16)) + tuple(
        g_ref[8 * v : 8 * v + 8, :] for v in range(16)
    )
    out = lax.fori_loop(first, last, body, init)
    for v in range(16):
        w_ref[8 * v : 8 * v + 8, :] = out[v]
        g_ref[8 * v : 8 * v + 8, :] = out[16 + v]


NAMES = (
    [a + b for a in ("P", "B", "C", "Y0", "Y1") for b in ("scatter", "y", "x", "turn", "z", "sib")]
    + [a + b for a in ("S", "Q0", "Q1") for b in ("sib", "z", "y", "x")]
    + [a + b for a in ("G0", "G1") for b in ("sib", "z", "back")]
)
NUMBER = {name: n for n, name in enumerate(NAMES)}


def kernel(
    h_ref,
    out_ref,
    xp,
    xb,
    xc,
    xy0,
    xy1,
    part0,
    part1,
    rs0,
    rs1,
    s_src,
    s_sib,
    s_z,
    s_gb,
    q0_src,
    q0_sib,
    q0_z,
    q0_gb,
    q1_src,
    q1_sib,
    q1_z,
    q1_gb,
    gsrc0,
    gsib0,
    gz0,
    gram0,
    gsrc1,
    gsib1,
    gz1,
    gram1,
    w_ref,
    g_ref,
    linv_ref,
    r_ref,
    vw,
    mid,
    send_sem,
    recv_sem,
):
    i = lax.axis_index("prow")
    k = lax.axis_index("pcol")
    y = k // NX
    x = k % NX
    z = i // 2
    core = i % 2
    sibling = (i + 1 - 2 * core, k)
    half = x // 2
    f_mine = (x % 2) * NY + y
    k_mine = i + PR * half
    home = k_mine == k
    mine = pl.ds(pl.multiple_of(f_mine * SL, SL), SL)
    turned = 2 * (f_mine % NZ) + f_mine // NZ
    turn_home = jnp.logical_and(home, turned == i)
    z_rows = pl.ds(pl.multiple_of((core * NZ + z) * SL, SL), SL)
    core_rows = pl.ds(pl.multiple_of(core * HF, HF), HF)
    other_rows = pl.ds(pl.multiple_of(HF - core * HF, HF), HF)

    def holder(f):
        return (k % PR, NX * (f % NY) + 2 * (k // PR) + f // NY)

    def y_mate(t):
        return (i, NX * lax.rem(y + 1 + t, NY) + x)

    def x_mate(t):
        return (i, NX * y + lax.rem(x + 1 + t, NX))

    def z_mate(t):
        return (lax.rem(i + 2 + 2 * t, PR), k)

    def send(src, dst, name, target):
        n = NUMBER[name]
        pltpu.make_async_remote_copy(
            src_ref=src,
            dst_ref=dst,
            send_sem=send_sem.at[n],
            recv_sem=recv_sem.at[n],
            device_id=target,
            device_id_type=MESH,
        ).start()

    def send_or_copy(src, dst, name, target):
        same = jnp.logical_and(target[0] == i, target[1] == k)

        @pl.when(same)
        def _():
            pltpu.make_async_copy(src, dst, recv_sem.at[NUMBER[name]]).start()

        @pl.when(jnp.logical_not(same))
        def _():
            send(src, dst, name, target)

    def loop(n, body):
        lax.fori_loop(0, n, lambda t, c: (body(t), c)[1], 0)

    def got(name, ref):
        pltpu.make_async_copy(ref, ref, recv_sem.at[NUMBER[name]]).wait()

    def sent(name, ref):
        pltpu.make_async_copy(ref, ref, send_sem.at[NUMBER[name]]).wait()

    def when(condition, body):
        @pl.when(condition)
        def _():
            body()

    barrier = pltpu.get_barrier_semaphore()

    def greet(target):
        same = jnp.logical_and(target[0] == i, target[1] == k)

        @pl.when(jnp.logical_not(same))
        def _():
            pl.semaphore_signal(barrier, inc=1, device_id=target, device_id_type=MESH)

    loop(PR, lambda t: greet(holder(t)))
    loop(PR, lambda t: greet((t, k_mine)))
    loop(NY - 1, lambda t: greet(y_mate(t)))
    loop(NX - 1, lambda t: greet(x_mate(t)))
    loop(NZ - 1, lambda t: greet(z_mate(t)))
    greet(sibling)
    others = (NY - 1) + (NX - 1) + (NZ - 1) + 1
    when(home, lambda: pl.semaphore_wait(barrier, others + 2 * (PR - 1)))
    when(jnp.logical_not(home), lambda: pl.semaphore_wait(barrier, others + 2 * PR))


    def scatter(ref, name):
        def body(t):
            rows = pl.ds(pl.multiple_of(t * SL, SL), SL)
            send_or_copy(h_ref.at[rows, :], ref.at[k // PR, rows, :], name + "scatter", holder(t))

        loop(PR, body)

    def along_y(ref, name):
        piece = ref.at[half, mine, :]
        loop(NY - 1, lambda t: send(piece, piece, name + "y", y_mate(t)))

    def along_x(ref, name):
        got(name + "y", ref.at[0, pl.ds(0, (NY - 1) * SL), :])
        run = ref.at[half, pl.ds(pl.multiple_of((x % 2) * HF, HF), HF), :]
        loop(NX - 1, lambda t: send(run, run, name + "x", x_mate(t)))

    def got_row(ref, name):
        got(name + "x", ref.at[pl.ds(0, 2), pl.ds(0, 3 * NB // 4), :])

    def turn(ref, name):
        send_or_copy(ref.at[half, mine, :], ref.at[2, mine, :], name + "turn", (turned, k_mine))

    def along_z(ref, name):
        piece = ref.at[2, z_rows, :]
        got(name + "turn", piece)
        loop(NZ - 1, lambda t: send(piece, piece, name + "z", z_mate(t)))

    def to_sibling(ref, name):
        got(name + "z", ref.at[2, pl.ds(0, (NZ - 1) * SL), :])
        run = ref.at[2, core_rows, :]
        send(run, run, name + "sib", sibling)

    def got_column(ref, name):
        got(name + "sib", ref.at[2, pl.ds(0, HF), :])


    def flow_start(name, src, sib):
        send(src, sib, name + "sib", sibling)

    def flow_z(name, src, sib, zb):
        got(name + "sib", sib)
        zb[z] = src[...] + sib[...]
        loop(NZ - 1, lambda t: send(zb.at[z], zb.at[z], name + "z", z_mate(t)))

    def flow_y(name, zb, gb):
        got(name + "z", zb.at[pl.ds(0, NZ - 1)])
        total = zb[0]
        for t in range(1, NZ):
            total += zb[t]
        rows = pl.ds(pl.multiple_of(y * SL, SL), SL)
        gb[x, rows, :] = total
        piece = gb.at[x, rows, :]
        loop(NY - 1, lambda t: send(piece, piece, name + "y", y_mate(t)))

    def flow_x(name, gb):
        got(name + "y", gb.at[0, pl.ds(0, (NY - 1) * SL), :])
        loop(NX - 1, lambda t: send(gb.at[x], gb.at[x], name + "x", x_mate(t)))

    def flow_end(name, gb):
        got(name + "x", gb.at[pl.ds(0, NX - 1)])

    def block(gb, n):
        lanes = slice(NB * n, NB * n + NB)
        return jnp.concatenate(
            [gb[0, :, lanes] + gb[2, :, lanes], gb[1, :, lanes] + gb[3, :, lanes]], axis=0
        )


    def gram_start(name, src, sib):
        send(src.at[other_rows, :], sib, name + "sib", sibling)

    def gram_z(name, src, sib, zb):
        got(name + "sib", sib)
        zb[z] = src[core_rows, :] + sib[...]
        loop(NZ - 1, lambda t: send(zb.at[z], zb.at[z], name + "z", z_mate(t)))

    def gram_back(name, zb, dst):
        got(name + "z", zb.at[pl.ds(0, NZ - 1)])
        total = zb[0]
        for t in range(1, NZ):
            total += zb[t]
        dst[core_rows, :] = total
        send(dst.at[core_rows, :], dst.at[core_rows, :], name + "back", sibling)

    def gram_end(name, dst):
        got(name + "back", dst.at[pl.ds(0, HF), :])

    def masked(value, index, j):
        lane = lax.broadcasted_iota(jnp.int32, value.shape, 1)
        return jnp.where(jnp.logical_and(lane < NB, index <= j), 0.0, value)

    def own_block(value, row):
        return jnp.where(jnp.logical_and(half == 0, i == row), value, 0.0)

    def reduce_scatter(part, buf, name):
        def body(t):
            rows = pl.ds(pl.multiple_of(t * SL, SL), SL)
            send_or_copy(part.at[rows, :], buf.at[i], name, holder(t))

        loop(PR, body)

    def times_matrix(rows):
        total = jnp.zeros((NB, CD), f32)
        for h in range(2):
            for m in range(4):
                lb = 2 * m + h
                total += dot_nn(rows[h][:, NB * m : NB * m + NB], h_ref[NB * lb : NB * lb + NB, :])
        return total

    def add_up(buf):
        total = buf[0]
        for t in range(1, PR):
            total += buf[t]
        return total

    when(i == 0, lambda: scatter(xp, "P"))
    when(i == 1, lambda: scatter(xb, "B"))
    when(i == 2, lambda: scatter(xc, "C"))

    got("Pscatter", xp.at[half, mine, :])
    along_y(xp, "P")
    turn(xp, "P")
    got("Bscatter", xb.at[half, mine, :])
    along_y(xb, "B")
    turn(xb, "B")
    got("Cscatter", xc.at[half, mine, :])
    along_y(xc, "C")
    turn(xc, "C")
    blocks = [(xp, 1), (xp, 2), (xb, 1), (xb, 2), (xc, 2)]
    for n, (ref, row) in enumerate(blocks):
        s_src[:, NB * n : NB * n + NB] = own_block(ref[half, mine, 0:NB], row)
    flow_start("S", s_src, s_sib)
    along_x(xp, "P")
    flow_z("S", s_src, s_sib, s_z)
    along_z(xp, "P")
    along_x(xb, "B")
    along_x(xc, "C")
    got_row(xp, "P")

    panel = [masked(xp[0], i, 0), xp[1]]
    part0[...] = times_matrix(panel)
    reduce_scatter(part0, rs0, "Y0scatter")
    gsrc0[...] = dot_nt(panel[0], panel[0]) + dot_nt(panel[1], panel[1])
    gram_start("G0", gsrc0, gsib0)
    flow_y("S", s_z, s_gb)
    along_z(xb, "B")
    along_z(xc, "C")
    gram_z("G0", gsrc0, gsib0, gz0)
    to_sibling(xp, "P")

    def image_pieces(rs, ref, name, j, q_src, rows):
        got(name + "scatter", rs)
        piece = add_up(rs)
        ref[half, mine, :] = piece
        along_y(ref, name)
        turn(ref, name)
        panel_half = jnp.where(half == 0, rows[0], rows[1])
        q_src[:, 0:NB] = dot_nt(piece, panel_half)
        for n, row in enumerate(range(j + 1, 3)):
            q_src[:, NB * (n + 1) : NB * (n + 2)] = own_block(piece[:, 0:NB], row)

    image_pieces(rs0, xy0, "Y0", 0, q0_src, panel)
    flow_start("Q0", q0_src, q0_sib)
    flow_x("S", s_gb)
    gram_back("G0", gz0, gram0)
    flow_z("Q0", q0_src, q0_sib, q0_z)
    along_x(xy0, "Y0")
    along_z(xy0, "Y0")
    gram_end("G0", gram0)
    flow_end("S", s_gb)

    w_ref[...] = gram0[...]
    g_ref[...] = block(s_gb, 0).T
    eliminate(0, 3, w_ref, g_ref, linv_ref, r_ref)
    flow_y("Q0", q0_z, q0_gb)
    eliminate(3, 8, w_ref, g_ref, linv_ref, r_ref)
    flow_x("Q0", q0_gb)
    to_sibling(xb, "B")
    to_sibling(xc, "C")
    to_sibling(xy0, "Y0")
    eliminate(8, 16, w_ref, g_ref, linv_ref, r_ref)

    def middle(quad, cross, corner):
        linv = linv_ref[...]
        coupling_t = dot_nn(r_ref[...], g_ref[...])
        mid[0] = dot_nn(linv, cross)
        mid[1] = dot_nt(dot_nn(linv, quad), linv)
        mid[2] = mid[0].T
        mid[3] = mid[1] + mid[0] + mid[2] + corner
        inner = dot_nt(dot_nn(coupling_t, mid[3]), coupling_t)
        return linv, coupling_t, inner

    def factors(mats, p, unit, image, e):
        linv, coupling_t, inner = mats
        vectors = dot_nn(linv, p) + unit
        weights = dot_nn(coupling_t, dot_nn(linv, image) + e) - 0.5 * dot_nn(inner, vectors)
        return vectors, weights

    def unit_at(condition, width):
        lane = lax.broadcasted_iota(jnp.int32, (NB, width), 1)
        row = lax.broadcasted_iota(jnp.int32, (NB, width), 0)
        return jnp.where(jnp.logical_and(lane == row, condition), 1.0, 0.0)

    flow_end("Q0", q0_gb)
    p_b = jnp.concatenate([block(s_gb, 0), block(s_gb, 1)], axis=1)
    b_b = jnp.concatenate([block(s_gb, 2), block(s_gb, 3)], axis=1)
    c_b2 = block(s_gb, 4)
    y_b = jnp.concatenate([block(q0_gb, 1), block(q0_gb, 2)], axis=1)
    mats = middle(block(q0_gb, 0), y_b[:, 0:NB], b_b[:, 0:NB])
    v_b, w_b = factors(mats, p_b, unit_at(True, 2 * NB), y_b, b_b)
    v_1, w_1 = v_b[:, 0:NB], w_b[:, 0:NB]
    v_2, w_2 = v_b[:, NB:], w_b[:, NB:]
    top1 = b_b[:, NB:] - dot_tn(w_1, v_2) - dot_tn(v_1, w_2)
    corner1 = c_b2 - dot_tn(w_2, v_2) - dot_tn(v_2, w_2)

    got_row(xb, "B")
    got_row(xy0, "Y0")
    got_row(xc, "C")
    for name, ref in (("P", xp), ("B", xb), ("C", xc), ("Y0", xy0)):
        got_column(ref, name)
    index = (i, PR, k)
    for s in range(3):
        p = xp[s] if s == 1 else masked(xp[s], index[s], 0)
        unit = 0.0 if s == 1 else unit_at(index[s] == 1, CD)
        v, w = factors(mats, p, unit, xy0[s], xb[s])
        vw[s, 0:NB, :] = v
        vw[s, NB : 2 * NB, :] = w

    next_panel, next_block = [], []
    for s in range(3):
        v, w = vw[s, 0:NB, :], vw[s, NB : 2 * NB, :]
        p = xb[s] - dot_tn(w_1, v) - dot_tn(v_1, w)
        next_panel.append(p if s == 1 else masked(p, index[s], 1))
        next_block.append(xc[s] - dot_tn(w_2, v) - dot_tn(v_2, w))

    rows = next_panel[0:2]
    across = dot_nt(rows[0], vw[0, 0 : 2 * NB, :]) + dot_nt(rows[1], vw[1, 0 : 2 * NB, :])
    part1[...] = (
        times_matrix(rows)
        - dot_nn(across[:, 0:NB], vw[2, NB : 2 * NB, :])
        - dot_nn(across[:, NB:], vw[2, 0:NB, :])
    )
    reduce_scatter(part1, rs1, "Y1scatter")
    gsrc1[...] = dot_nt(rows[0], rows[0]) + dot_nt(rows[1], rows[1])
    gram_start("G1", gsrc1, gsib1)
    gram_z("G1", gsrc1, gsib1, gz1)
    image_pieces(rs1, xy1, "Y1", 1, q1_src, rows)
    flow_start("Q1", q1_src, q1_sib)
    gram_back("G1", gz1, gram1)
    flow_z("Q1", q1_src, q1_sib, q1_z)
    along_x(xy1, "Y1")
    along_z(xy1, "Y1")
    gram_end("G1", gram1)
    w_ref[...] = gram1[...]
    g_ref[...] = top1.T
    eliminate(0, 3, w_ref, g_ref, linv_ref, r_ref)
    flow_y("Q1", q1_z, q1_gb)
    eliminate(3, 8, w_ref, g_ref, linv_ref, r_ref)
    flow_x("Q1", q1_gb)
    to_sibling(xy1, "Y1")
    eliminate(8, 16, w_ref, g_ref, linv_ref, r_ref)
    flow_end("Q1", q1_gb)
    mats = middle(block(q1_gb, 0), block(q1_gb, 1), corner1)
    got_row(xy1, "Y1")
    got_column(xy1, "Y1")
    for s in range(3):
        unit = 0.0 if s == 1 else unit_at(index[s] == 2, CD)
        v, w = factors(mats, next_panel[s], unit, xy1[s], next_block[s])
        vw[s, 2 * NB : 3 * NB, :] = v
        vw[s, 3 * NB : 4 * NB, :] = w

    right = jnp.concatenate(
        [vw[2, NB * n : NB * n + NB, :] for n in (1, 0, 3, 2)], axis=0
    )
    for h in range(2):
        for m in range(4):
            lb = NB * (2 * m + h)
            update = dot_tn(vw[h, :, NB * m : NB * m + NB], right)
            out_ref[lb : lb + NB, :] = h_ref[lb : lb + NB, :] - update

    def sent_pieces(name):
        when(home, lambda: sent(name, xp.at[0, pl.ds(0, NB - SL), :]))
        when(jnp.logical_not(home), lambda: sent(name, xp.at[0]))

    when(i == 0, lambda: sent_pieces("Pscatter"))
    when(i == 1, lambda: sent_pieces("Bscatter"))
    when(i == 2, lambda: sent_pieces("Cscatter"))
    sent_pieces("Y0scatter")
    sent_pieces("Y1scatter")
    for name in ("P", "B", "C", "Y0", "Y1"):
        sent(name + "y", xp.at[0, pl.ds(0, (NY - 1) * SL), :])
        sent(name + "x", xp.at[pl.ds(0, 2), pl.ds(0, 3 * NB // 4), :])
        when(
            jnp.logical_not(turn_home),
            lambda name=name: sent(name + "turn", xp.at[0, pl.ds(0, SL), :]),
        )
        sent(name + "z", xp.at[0, pl.ds(0, (NZ - 1) * SL), :])
        sent(name + "sib", xp.at[0, pl.ds(0, HF), :])
    for name, sib, zb, gb in (
        ("S", s_sib, s_z, s_gb),
        ("Q0", q0_sib, q0_z, q0_gb),
        ("Q1", q1_sib, q1_z, q1_gb),
    ):
        sent(name + "sib", sib)
        sent(name + "z", zb.at[pl.ds(0, NZ - 1)])
        sent(name + "y", gb.at[0, pl.ds(0, (NY - 1) * SL), :])
        sent(name + "x", gb.at[pl.ds(0, NX - 1)])
    for name, sib, zb, dst in (("G0", gsib0, gz0, gram0), ("G1", gsib1, gz1, gram1)):
        sent(name + "sib", sib)
        sent(name + "z", zb.at[pl.ds(0, NZ - 1)])
        sent(name + "back", dst.at[pl.ds(0, HF), :])


def on_device(matrix):
    vmem = pl.BlockSpec(memory_space=pltpu.VMEM)

    def flow(width):
        return [
            pltpu.VMEM((SL, width), f32),
            pltpu.VMEM((SL, width), f32),
            pltpu.VMEM((NZ, SL, width), f32),
            pltpu.VMEM((NX, HF, width), f32),
        ]

    def gram():
        return [
            pltpu.VMEM((NB, NB), f32),
            pltpu.VMEM((HF, NB), f32),
            pltpu.VMEM((NZ, HF, NB), f32),
            pltpu.VMEM((NB, NB), f32),
        ]

    return pl.pallas_call(
        kernel,
        out_shape=jax.ShapeDtypeStruct(matrix.shape, f32),
        in_specs=[vmem],
        out_specs=vmem,
        scratch_shapes=(
            [pltpu.VMEM((3, NB, CD), f32)] * 5
            + [pltpu.VMEM((NB, CD), f32)] * 2
            + [pltpu.VMEM((PR, SL, CD), f32)] * 2
            + flow(5 * NB)
            + flow(3 * NB)
            + flow(2 * NB)
            + gram()
            + gram()
            + [pltpu.VMEM((NB, NB), f32)] * 4
            + [pltpu.VMEM((3, 4 * NB, CD), f32), pltpu.VMEM((4, NB, NB), f32)]
            + [pltpu.SemaphoreType.DMA((len(NAMES),))] * 2
        ),
        compiler_params=pltpu.CompilerParams(
            collective_id=0, has_side_effects=True, vmem_limit_bytes=48 * 1024 * 1024
        ),
        name="band_reduction",
    )(matrix)


def solution(mesh):
    return jax.shard_map(
        on_device,
        mesh=mesh,
        in_specs=(P("prow", "pcol"),),
        out_specs=P("prow", "pcol"),
        check_vma=False,
    )
```

time: 1640 us -> 148 us (0.09)
  waiting for transfers between devices: 1470 us -> 0 us
  Pallas kernels: 0 us -> 145 us
  other arithmetic: 103 us -> 0 us
  matrix products: 34.3 us -> 0 us
    psum x12 -> x0, waiting for transfers between devices: 1470 us -> none  [the longest x6 763 us: broadcast(): return lax.psum(block, axis)]
    pallas_call x0 -> x1, Pallas kernels: none -> 145 us  [on_device(): pl.pallas_call(kernel, out_shape=jax.ShapeDtypeStruct(matrix.shape, f32),...]
    another operation x20 -> x0, other arithmetic: 91.5 us -> none  [the longest x6 24.9 us: on_device(): factor = jnp.linalg.cholesky(inner_product(shifted, shifted))]
    dot_general x20 -> x0, matrix products: 32.8 us -> none  [the longest x6 12.4 us: product_of(): jnp.dot(left, right, precision=exact_mode, preferred_element_type=jnp.flo...]
  transfers between devices with their start and end apart: 12 -> 0, of which waited for: 12 -> 0; matrix products, arithmetic and copies ran while one was open for 1% -> 0% of each run, Pallas kernels for 0% -> 0%
where the time goes in v2:
time: 148 us
  Pallas kernels  145 us (98%)
  local copies, waits for them, and re-layouts  2.91 us (2%)
    pallas_call x1, Pallas kernels, on_device(): pl.pallas_call(kernel, out_shape=jax.ShapeDtypeStruct(matrix.shape, f32),...  145 us

profile of v2, /device:TPU:1, one launch (start us, length us, event | category | flops | bytes accessed | tf_op | source)
XLA Modules:
  0.0 147.7 jit_solution(7460048669402008060)
XLA Ops:
  0.0 0.0 copy-start
  0.0 1.6 %copy-done = f32[1024,512]{1,0:T(8,128)S(1)} copy-done((f32[1024,512]{1,0:T(8,128)S(1)}, f32[1024,512]{1,0:T(8,128)}, u32[]{:S(2)}) %copy-start) | copy-done | bytes 2097176
  1.6 144.7 %band_reduction.1 = f32[1024,512]{1,0:T(8,128)S(1)} custom-call(f32[1024,512]{1,0:T(8,128)S(1)} %copy-done), custom_call_target="tpu_custom_call" | custom-call | tf_op jit(solution)/shard_map/band_reduction/pallas_call | solution.py:556
  146.3 1.3 copy.3
Async XLA Ops:
  0.0 1.6 %copy-start = (f32[1024,512]{1,0:T(8,128)S(1)}, f32[1024,512]{1,0:T(8,128)}, u32[]{:S(2)}) copy-start(f32[1024,512]{1,0:T(8,128)} %h_ref.1) | copy-start | bytes 6291460
